TPU v7x, 256 devices: a whole 4x4x8 slice. The times are simulated.
256 devices in a mesh: grp: 2 (over core), beam: 8 (over z_lo, y), row: 16 (over x, z_hi).
Axes of the slice: x: 4, y: 4, z: 8 (z_hi: 4, z_lo: 2; z = z_hi * 2 + z_lo), core: 2. Of those that a mesh axis runs over, the one named last changes fastest.
Arguments:
- densities: bfloat16 [32, 256, 32, 2048], P(None, 'grp', 'beam', 'row'), may hold values from 0 to 1
- spectra: bfloat16 [256, 2048, 512], P(('grp', 'beam'), 'row'), may hold values from -6 to 6
- intensities: bfloat16 [8192, 4096], P(('grp', 'beam', 'row')), may hold values from 0.099609375 to 4
- positions: int32 [8192, 2], P(('grp', 'beam', 'row')), may hold values from 0 to 64, as said below
- probe: float32 [2, 4096], replicated, may hold values from -6 to 6
- line_channels: int32 [32, 4], replicated, may hold values from 0 to 511
- line_weights: float32 [32, 4], replicated, may hold values from 0.2 to 1
- atten_coef: float32 [32], replicated, may hold values from 0.00048828125 to 0.00390625
- beta_coef: float32 [32], replicated, may hold values from 0.0001953125 to 0.001953125
- delta_coef: float32 [32], replicated, may hold values from 0.0009765625 to 0.0078125
Outputs:
- density_grad: bfloat16 [32, 256, 32, 2048], P(None, 'grp', 'beam', 'row')
- probe_grad: float32 [2, 4096], replicated
Inputs may be any that keep to these rules, and one draw needn't show every extreme that they name: `positions`: column 0 is within 0 to 64, column 1 within 0 to 64; each device's first position has the largest layer offset and its second the largest row offset.
All inputs are finite; a program needn't handle non-finite values.
Results may differ from a plain program's by a relative error of at most 0.001.
Values sent between devices are 32-bit elements; how exact they have to be, the bound alone decides.
A program may use at most 128 MiB of HBM per device.

v0:
```python
import functools
import math

import jax
import jax.numpy as jnp
import numpy as np
from jax import lax
from jax.experimental import pallas as pl
from jax.experimental.pallas import tpu as pltpu
from jax.sharding import PartitionSpec as P

E = 32
C = 512
M = 64
K = 32
X = 4
ZB = 16
NB = 8
GROUP = 16
NEAREST = (4, 1, 7, 3, 5, 2, 6)
ORDER = tuple((step, half) for half in range(2) for step in NEAREST)
EARLY = 3
PART = 4

F32 = jnp.float32
BF16 = jnp.bfloat16
HIGHEST = lax.Precision.HIGHEST
MESH = pl.DeviceIdType.MESH
object_weight = 1000.0


def halves(values):
    high = values.astype(BF16)
    return high, (values - high.astype(F32)).astype(BF16)


def swap(values):
    return pltpu.roll(values, M, 1)


def matmul(left, right):
    return jnp.dot(left, right, preferred_element_type=F32)


def np_halves(values):
    high = values.astype(np.float32).astype(jnp.bfloat16)
    low = (values - high.astype(np.float64)).astype(np.float32).astype(jnp.bfloat16)
    return high, low


def constant_tables():
    index = np.arange(M)
    angles = 2.0 * math.pi / M * (index[:, None] * index[None, :] % M)
    dft_real = np.cos(angles) / math.sqrt(M)
    dft_imag = -np.sin(angles) / math.sqrt(M)
    centred = np.arange(M) - M // 2
    chirp = math.pi * 0.5 / M * (centred[:, None] ** 2 + centred[None, :] ** 2)
    chirp_real, chirp_imag = np.cos(chirp), np.sin(chirp)
    chirps = np.stack(
        [
            np.concatenate([chirp_real, chirp_real], 1),
            np.concatenate([-chirp_imag, chirp_imag], 1),
        ]
    ).astype(np.float32)

    def right_table(sign):
        table = np.block([[dft_real, sign * dft_imag], [-sign * dft_imag, dft_real]])
        high, low = np_halves(table)
        row = np.concatenate([high, low], 1)
        return np.concatenate([row, row], 0)

    right = np.stack([right_table(1.0), right_table(-1.0)])
    high, low = np_halves(np.concatenate([dft_real, dft_imag], 0))
    left = np.concatenate([high, high, low, low], 1)
    return chirps, right, left


def kernel(
    sizes,
    dens_hbm,
    spec_hbm,
    inten_hbm,
    pos_ref,
    probe_ref,
    chan_ref,
    weight_ref,
    atten_ref,
    beta_ref,
    delta_ref,
    chirp_ref,
    right_ref,
    left_ref,
    out_hbm,
    probe_out,
    dens_bf,
    dens_f,
    spec_v,
    inten_bf,
    inten_f,
    image_ref,
    tap_src,
    tap_rcv,
    u_src,
    u_rcv,
    ow_src,
    ow_rcv,
    inc_ref,
    tg_src,
    tg_rcv,
    lg_src,
    lg_rcv,
    eg_ref,
    mix_ref,
    fit_ref,
    out_v,
    tile_ref,
    pgsum_ref,
    pr_src,
    pr_rcv,
    pa_rcv,
    pb_rcv,
    pf_rcv,
    dens_sem,
    spec_sem,
    inten_sem,
    out_sem,
    tap_ss,
    tap_rs,
    u_ss,
    u_rs,
    ow_ss,
    ow_rs,
    tg_ss,
    tg_rs,
    lg_ss,
    lg_rs,
    eg_ss,
    eg_rs,
    pr_ss,
    pr_rs,
    pa_ss,
    pa_rs,
    pb_ss,
    pb_rs,
    pf_ss,
    pf_rs,
):
    n_grp, n_row, n_x, n_zh, total = sizes
    me = lax.axis_index("beam")
    grp = lax.axis_index("grp")
    row = lax.axis_index("row")
    row_x, row_z = row // n_zh, row % n_zh
    n_near = n_grp * n_zh
    near = grp * n_zh + row_z

    def near_id(step):
        other = (near + step) % n_near
        return {"grp": other // n_zh, "row": row_x * n_zh + other % n_zh}

    def x_id(step):
        return {"row": ((row_x + step) % n_x) * n_zh + row_z}

    def peer(step):
        return (me + step) % NB

    def remote(source, target, send, recv, device):
        return pltpu.make_async_remote_copy(
            src_ref=source,
            dst_ref=target,
            send_sem=send,
            recv_sem=recv,
            device_id=device,
            device_id_type=MESH,
        )

    barrier = pltpu.get_barrier_semaphore()
    for step in range(1, NB):
        pl.semaphore_signal(barrier, inc=1, device_id={"beam": peer(step)}, device_id_type=MESH)
    for step in range(1, n_near):
        pl.semaphore_signal(barrier, inc=1, device_id=near_id(step), device_id_type=MESH)
    for step in range(1, n_x):
        pl.semaphore_signal(barrier, inc=1, device_id=x_id(step), device_id_type=MESH)

    def dens_copy(step):
        block = (me + 1 + step) % NB
        return pltpu.make_async_copy(
            dens_hbm.at[:, block], dens_bf.at[:, block], dens_sem.at[step]
        )

    for step in range(NB):
        dens_copy(step).start()
    spec_copy = pltpu.make_async_copy(spec_hbm, spec_v, spec_sem)
    spec_copy.start()
    inten_copy = pltpu.make_async_copy(inten_hbm, inten_bf, inten_sem)
    inten_copy.start()

    def cell(e, block, x):
        return dens_f[e, block, pl.ds(x, ZB, stride=X), :]

    def project(step, carry):
        block = (me + 1 + step) % NB
        dens_copy(step).wait()
        dens_f[:, block] = dens_bf[:, block].astype(F32)

        def add(e, sums):
            cells = [cell(e, block, x) for x in range(X)]
            total_cells = (cells[0] + cells[1]) + (cells[2] + cells[3])
            optical = [sums[x] + atten_ref[e] * cells[x] for x in range(X)]
            return (
                *optical,
                sums[X] + beta_ref[e] * total_cells,
                sums[X + 1] + delta_ref[e] * total_cells,
            )

        zero = jnp.zeros((ZB, 128), F32)
        sums = lax.fori_loop(0, E, add, (zero,) * (X + 2), unroll=E)
        depth = zero
        for x in range(X):
            inc_ref[block, x] = jnp.exp(-depth)
            depth = depth + sums[x]
        tap_src[block, 0] = depth
        tap_src[block, 1] = sums[X]
        tap_src[block, 2] = sums[X + 1]

        return carry

    lax.fori_loop(0, NB, project, 0)
    pl.semaphore_wait(barrier, NB - 1 + n_near - 1 + n_x - 1)
    tap_sends, u_sends = [], []

    def send_tap(step):
        dst = peer(step)
        copy = remote(
            tap_src.at[dst], tap_rcv.at[me], tap_ss.at[step], tap_rs.at[me], {"beam": dst}
        )
        copy.start()
        tap_sends.append(copy)

    def u_copy(step, half):
        dst = peer(step)
        return remote(
            u_src.at[dst, half],
            u_rcv.at[me, half],
            u_ss.at[step, half],
            u_rs.at[me, half],
            {"beam": dst},
        )

    def send_u(step, half):
        copy = u_copy(step, half)
        copy.start()
        u_sends.append(copy)

    def wait_u(half):
        for step in range(1, NB):
            src = peer(step)
            remote(
                u_src.at[src, half],
                u_rcv.at[src, half],
                u_ss.at[step, half],
                u_rs.at[src, half],
                {"beam": src},
            ).wait_recv()

    for step in range(1, NB):
        send_tap(step)
    tap_rcv[me] = tap_src[me]

    def emit(step, carry):
        block = (me + 1 + step) % NB
        local = [inc_ref[block, x] for x in range(X)]

        def one(e, inner):
            terms = [cell(e, block, x) * local[x] for x in range(1, X)]
            value = (cell(e, block, 0) + terms[0]) + (terms[1] + terms[2])
            u_src[block, 0, e] = value[:8]
            u_src[block, 1, e] = value[8:]
            return inner

        lax.fori_loop(0, E, one, 0, unroll=E)

        return carry

    lax.fori_loop(0, NB, emit, 0)
    for step, half in ORDER[:EARLY]:
        send_u(step, half)
    u_rcv[me] = u_src[me]

    for step in range(1, NB):
        src = peer(step)
        remote(tap_src.at[src], tap_rcv.at[src], tap_ss.at[0], tap_rs.at[src], {"beam": src}).wait_recv()
    before = jnp.zeros((ZB, 128), F32)
    absorb = jnp.zeros((ZB, 128), F32)
    phase = jnp.zeros((ZB, 128), F32)
    for d in range(NB):
        ow_src[d, 2] = jnp.exp(-before)
        before = before + tap_rcv[d, 0]
        absorb = absorb + tap_rcv[d, 1]
        phase = phase + tap_rcv[d, 2]
    amplitude = jnp.exp(-absorb)
    own_real = amplitude * jnp.cos(phase)
    own_imag = amplitude * jnp.sin(phase)
    for d in range(NB):
        ow_src[d, 0] = own_real
        ow_src[d, 1] = own_imag
    ow_sends = []
    for step in range(1, NB):
        dst = peer(step)
        copy = remote(
            ow_src.at[dst], ow_rcv.at[me], ow_ss.at[step], ow_rs.at[me], {"beam": dst}
        )
        copy.start()
        ow_sends.append(copy)
    ow_rcv[me] = ow_src[me]
    for step, half in ORDER[EARLY:]:
        send_u(step, half)

    eye = (
        lax.broadcasted_iota(jnp.int32, (E, E), 0) == lax.broadcasted_iota(jnp.int32, (E, E), 1)
    ).astype(F32)

    def columns_of(rows):
        return lax.dot_general(
            eye, rows, (((1,), (1,)), ((), ())), precision=HIGHEST, preferred_element_type=F32
        )

    lines = columns_of(chan_ref[...].astype(F32))
    strengths = columns_of(weight_ref[...])
    channel = lax.broadcasted_iota(jnp.int32, (E, C), 1).astype(F32)
    table = jnp.zeros((E, C), F32)
    for line in range(4):
        offset = channel - lines[:, line : line + 1]
        table = table + strengths[:, line : line + 1] * jnp.exp(-offset * offset / 8.0)
    gram = lax.dot_general(
        table, table, (((1,), (1,)), ((), ())), precision=HIGHEST, preferred_element_type=F32
    )
    gram_high, gram_low = halves(gram)
    gram_parts = jnp.concatenate([gram_high, gram_low], 0)

    spec_copy.wait()
    table_high, table_low = halves(table)
    fit = lax.dot_general(
        jnp.concatenate([table_high, table_low], 0),
        spec_v[...],
        (((1,), (1,)), ((), ())),
        preferred_element_type=F32,
    )
    fit_ref[...] = fit[:E] + fit[E:]

    lane = lax.broadcasted_iota(jnp.int32, (M, 128), 1)
    first = lane < M
    even = lax.broadcasted_iota(jnp.int32, (M, 128), 0) % 2 == 0
    inten_copy.wait()
    flat = inten_bf[...].astype(F32)
    for g in range(M // 2):
        group = flat[:, g * 128 : (g + 1) * 128]
        inten_f[pl.ds(2 * g, K, stride=M), :] = group
        inten_f[pl.ds(2 * g + 1, K, stride=M), :] = group
    for part in range(2):
        for g in range(M // 2):
            group = probe_ref[part : part + 1, g * 128 : (g + 1) * 128]
            image_ref[part, 2 * g : 2 * g + 1, :] = group
            image_ref[part, 2 * g + 1 : 2 * g + 2, :] = group
    image_real, image_imag = image_ref[0], image_ref[1]
    probe = jnp.where(
        first,
        jnp.where(even, image_real, swap(image_real)),
        jnp.where(even, swap(image_imag), image_imag),
    )
    keep = first == even

    for step in range(1, NB):
        src = peer(step)
        remote(ow_src.at[src], ow_rcv.at[src], ow_ss.at[0], ow_rs.at[src], {"beam": src}).wait_recv()

    illum = probe * chirp_ref[0] + swap(probe) * chirp_ref[1]
    illum_swap = swap(illum)
    illum_a = jnp.where(first, illum, illum_swap)
    illum_b = jnp.where(first, -illum_swap, illum)
    sign = jnp.where(first, -1.0, 1.0).astype(F32)

    obj_real = ow_rcv[:, 0].reshape(NB * ZB, 128)
    obj_imag = ow_rcv[:, 1].reshape(NB * ZB, 128)
    real_high, real_low = halves(obj_real)
    imag_high, imag_low = halves(obj_imag)
    field = jnp.concatenate([real_high, imag_high, real_low, imag_low], 1)

    pick_z = lax.broadcasted_iota(jnp.int32, (M, 128), 1) - lax.broadcasted_iota(
        jnp.int32, (M, 128), 0
    )
    gather_row = lax.broadcasted_iota(jnp.int32, (256, 128), 0)
    gather_col = lax.broadcasted_iota(jnp.int32, (256, 128), 1)
    pick_y = jnp.where(
        (gather_row < 128) == (gather_col < M), gather_row % 128 - gather_col % M, -1
    )
    spread_row = lax.broadcasted_iota(jnp.int32, (128, 256), 0)
    spread_col = lax.broadcasted_iota(jnp.int32, (128, 256), 1)
    place_y = jnp.where(
        (spread_col < 128) == (spread_row < M), spread_col % 128 - spread_row % M, -1
    )
    place_z = lax.broadcasted_iota(jnp.int32, (128, 128), 0) - (
        lax.broadcasted_iota(jnp.int32, (128, 128), 1) % M
    )

    tile_ref[...] = jnp.zeros(tile_ref.shape, F32)
    pgsum_ref[...] = jnp.zeros(pgsum_ref.shape, F32)

    def transform(values, right, conj):
        high, low = halves(values)
        product = matmul(jnp.concatenate([high, low], 1), right)
        product = product[:, :128] + product[:, 128:]
        high, low = halves(product)
        outs = []
        for i in range(GROUP):
            part = slice(i * M, (i + 1) * M)
            stack = jnp.concatenate([high[part], low[part], high[part], low[part]], 0)
            both = matmul(left_ref[...], stack)
            turned = swap(both[M:]) * sign
            outs.append(both[:M] - turned if conj else both[:M] + turned)
        return outs

    def positions_step(group, carry):
        windows, picks = [], []
        starts = [
            (pos_ref[0, group * GROUP + i], pos_ref[1, group * GROUP + i])
            for i in range(GROUP)
        ]
        for i in range(GROUP):
            rows = (pick_z == starts[i][0]).astype(F32).astype(BF16)
            cut = matmul(rows, field).astype(BF16)
            stack = jnp.concatenate([cut[:, :256], cut[:, 256:]], 0)
            columns = (pick_y == starts[i][1]).astype(F32).astype(BF16)
            both = matmul(stack, columns)
            windows.append(both[:M] + both[M:])
        exits = [w * illum_a + swap(w) * illum_b for w in windows]
        far = transform(jnp.concatenate(exits, 0), right_ref[0], False)
        pulled = []
        for i in range(GROUP):
            square = far[i] * far[i]
            start = pl.multiple_of((group * GROUP + i) * M, M)
            measured = inten_f[pl.ds(start, M), :]
            measured = jnp.where(keep, measured, swap(measured))
            misfit = square + swap(square) - measured
            pulled.append(misfit * far[i])
        back = transform(jnp.concatenate(pulled, 0), right_ref[1], True)
        sum_a = pgsum_ref[0]
        sum_b = pgsum_ref[1]
        tile = tile_ref[...]
        for i in range(GROUP):
            sum_a = sum_a + windows[i] * back[i]
            sum_b = sum_b + swap(windows[i]) * back[i]
            grad = back[i] * illum_a - swap(back[i]) * illum_b
            high, low = halves(grad)
            columns = (place_y == starts[i][1]).astype(F32).astype(BF16)
            spread = matmul(jnp.concatenate([high, low], 0), columns).astype(BF16)
            rows = (place_z == starts[i][0]).astype(F32).astype(BF16)
            tile = tile + matmul(rows, spread)
        pgsum_ref[0] = sum_a
        pgsum_ref[1] = sum_b
        tile_ref[...] = tile
        return carry

    lax.fori_loop(0, K // GROUP, positions_step, 0)

    for d in range(NB):
        tg_src[d, 0] = tile_ref[d * ZB : (d + 1) * ZB, :128]
        tg_src[d, 1] = tile_ref[d * ZB : (d + 1) * ZB, 128:]
    sum_a, sum_b = pgsum_ref[0], pgsum_ref[1]
    conj_sum = jnp.where(first, sum_a + swap(sum_a), sum_b - swap(sum_b))
    local_probe = conj_sum * chirp_ref[0] - swap(conj_sum) * chirp_ref[1]
    image_ref[0] = local_probe
    upper, lower = image_ref[0, pl.ds(0, M // 2, stride=2), :], image_ref[0, pl.ds(1, M // 2, stride=2), :]
    half_first = first[: M // 2]
    flat_real = jnp.where(half_first, upper, swap(lower))
    flat_imag = jnp.where(half_first, swap(upper), lower)
    for d in range(NB // 2):
        pr_src[d] = flat_real[d * 8 : (d + 1) * 8]
        pr_src[NB // 2 + d] = flat_imag[d * 8 : (d + 1) * 8]
    tg_sends, pr_sends = [], []
    for step in range(1, NB):
        dst = peer(step)
        copy = remote(
            tg_src.at[dst], tg_rcv.at[me], tg_ss.at[step], tg_rs.at[me], {"beam": dst}
        )
        copy.start()
        tg_sends.append(copy)
    for step in range(1, NB):
        dst = peer(step)
        copy = remote(
            pr_src.at[dst], pr_rcv.at[me], pr_ss.at[step], pr_rs.at[me], {"beam": dst}
        )
        copy.start()
        pr_sends.append(copy)
    tg_rcv[me] = tg_src[me]
    pr_rcv[me] = pr_src[me]

    def scale_block(block, carry):
        for x in range(X):
            inc_ref[block, x] = inc_ref[block, x] * ow_rcv[block, 2]
        return carry

    lax.fori_loop(0, NB, scale_block, 0)

    shield = [ow_src[d, 2] for d in range(NB)]

    def own_half(half):
        rows = slice(half * 8, half * 8 + 8)
        count = E * 8

        def add_slabs(e, carry):
            value = u_rcv[0, half, e] * shield[0][rows]
            for d in range(1, NB):
                value = value + u_rcv[d, half, e] * shield[d][rows]
            mix_ref[pl.ds(half * count + e, 8, stride=E), :] = value
            return carry

        lax.fori_loop(0, E, add_slabs, 0, unroll=E)
        columns = jnp.concatenate(
            [mix_ref[half * count + z * E : half * count + (z + 1) * E, :] for z in range(8)], 1
        )
        high, low = halves(columns)
        product = matmul(gram_parts, jnp.concatenate([high, low], 1))
        product = product[:E] + product[E:]
        grads = (product[:, :1024] + product[:, 1024:]) - fit_ref[:, half * 1024 : half * 1024 + 1024]
        for z in range(8):
            mix_ref[half * count + z * E : half * count + (z + 1) * E, :] = grads[
                :, z * 128 : (z + 1) * 128
            ]

        def to_layers(e, carry):
            eg_ref[me, half, e] = mix_ref[pl.ds(half * count + e, 8, stride=E), :]
            return carry

        lax.fori_loop(0, E, to_layers, 0, unroll=E)

    beam_z, beam_y = me // 4, me % 4
    up = beam_z * 4 + (beam_y + 1) % 4
    down = beam_z * 4 + (beam_y + 3) % 4
    across = (1 - beam_z) * 4 + beam_y
    far_side = beam_z * 4 + (beam_y + 2) % 4
    across_up = (1 - beam_z) * 4 + (beam_y + 1) % 4
    across_down = (1 - beam_z) * 4 + (beam_y + 3) % 4
    across_far = (1 - beam_z) * 4 + (beam_y + 2) % 4

    eg_sends = []

    def hand(block, half, dst):
        copy = remote(
            eg_ref.at[block, half],
            eg_ref.at[block, half],
            eg_ss.at[len(eg_sends)],
            eg_rs.at[block, half],
            {"beam": dst},
        )
        copy.start()
        eg_sends.append(copy)

    def arrive(block, half):
        remote(
            eg_ref.at[block, half],
            eg_ref.at[block, half],
            eg_ss.at[0],
            eg_rs.at[block, half],
            {"beam": block},
        ).wait_recv()

    wait_u(0)
    own_half(0)
    hand(me, 0, up)
    hand(me, 0, across)
    hand(me, 0, down)
    wait_u(1)
    for step in range(1, NB):
        src = peer(step)
        remote(pr_src.at[src], pr_rcv.at[src], pr_ss.at[0], pr_rs.at[src], {"beam": src}).wait_recv()
    piece = pr_rcv[0]
    for d in range(1, NB):
        piece = piece + pr_rcv[d]
    pa_rcv[near] = piece
    pa_sends = []
    for step in range(1, n_near):
        copy = remote(
            pa_rcv.at[near], pa_rcv.at[near], pa_ss.at[step], pa_rs.at[near], near_id(step)
        )
        copy.start()
        pa_sends.append(copy)
    own_half(1)
    hand(me, 1, down)
    hand(me, 1, across)
    hand(me, 1, up)

    def weigh(e, sums):
        value = jnp.concatenate([eg_ref[me, 0, e], eg_ref[me, 1, e]], 0)
        return tuple(
            sums[d] + value * jnp.concatenate([u_rcv[d, 0, e], u_rcv[d, 1, e]], 0)
            for d in range(NB)
        )

    weighted = lax.fori_loop(0, E, weigh, (jnp.zeros((ZB, 128), F32),) * NB, unroll=8)

    for step in range(1, NB):
        src = peer(step)
        remote(tg_src.at[src], tg_rcv.at[src], tg_ss.at[0], tg_rs.at[src], {"beam": src}).wait_recv()
    tile_real = tg_rcv[0, 0]
    tile_imag = tg_rcv[0, 1]
    for d in range(1, NB):
        tile_real = tile_real + tg_rcv[d, 0]
        tile_imag = tile_imag + tg_rcv[d, 1]
    own_real, own_imag = ow_src[0, 0], ow_src[0, 1]
    grad_absorb = -object_weight * (own_real * tile_real + own_imag * tile_imag)
    grad_phase = object_weight * (own_real * tile_imag - own_imag * tile_real)
    later = jnp.zeros((ZB, 128), F32)
    for d in range(NB - 1, -1, -1):
        lg_src[d, 0] = later
        lg_src[d, 1] = grad_absorb
        lg_src[d, 2] = grad_phase
        later = later + weighted[d] * shield[d]
    lg_sends = []
    for step in range(1, NB):
        dst = peer(step)
        copy = remote(
            lg_src.at[dst], lg_rcv.at[me], lg_ss.at[step], lg_rs.at[me], {"beam": dst}
        )
        copy.start()
        lg_sends.append(copy)
    lg_rcv[me] = lg_src[me]

    def out_copy(order, block):
        return pltpu.make_async_copy(
            out_v.at[:, block], out_hbm.at[:, block], out_sem.at[order]
        )

    def finish(order, block):
        def grad_of(e):
            return jnp.concatenate([eg_ref[block, 0, e], eg_ref[block, 1, e]], 0)

        def weigh_cells(e, sums):
            value = grad_of(e)
            return tuple(sums[x] + value * cell(e, block, x) for x in range(X))

        zero = jnp.zeros((ZB, 128), F32)
        sums = lax.fori_loop(0, E, weigh_cells, (zero,) * X, unroll=E)
        light = [inc_ref[block, x] for x in range(X)]
        beyond = [None] * X
        running = lg_rcv[block, 0]
        for x in range(X - 1, -1, -1):
            beyond[x] = running
            running = running + light[x] * sums[x]
        absorb_grad, phase_grad = lg_rcv[block, 1], lg_rcv[block, 2]

        def write(e, carry):
            value = grad_of(e)
            shared = beta_ref[e] * absorb_grad + delta_ref[e] * phase_grad
            for x in range(X):
                result = value * light[x] - atten_ref[e] * beyond[x] + shared
                dens_f[e, block, pl.ds(x, ZB, stride=X), :] = result
            out_v[e, block] = dens_f[e, block].astype(BF16)
            return carry

        lax.fori_loop(0, E, write, 0, unroll=E)
        out_copy(order, block).start()

    def extras(block):
        remote(lg_src.at[block], lg_rcv.at[block], lg_ss.at[0], lg_rs.at[block], {"beam": block}).wait_recv()

    arrive(down, 0)
    hand(down, 0, up)
    arrive(across, 0)
    hand(across, 0, up)
    hand(across, 0, down)
    arrive(up, 1)
    hand(up, 1, down)
    arrive(across, 1)
    hand(across, 1, up)
    hand(across, 1, down)
    finish(0, me)

    for step in range(1, n_near):
        src = (near + step) % n_near
        remote(pa_rcv.at[src], pa_rcv.at[src], pa_ss.at[0], pa_rs.at[src], near_id(step)).wait_recv()
    piece = pa_rcv[0]
    for d in range(1, n_near):
        piece = piece + pa_rcv[d]
    pb_rcv[row_x] = piece
    pb_sends = []
    for step in range(1, n_x):
        copy = remote(
            pb_rcv.at[row_x], pb_rcv.at[row_x], pb_ss.at[step], pb_rs.at[row_x], x_id(step)
        )
        copy.start()
        pb_sends.append(copy)

    arrive(down, 1)
    extras(down)
    finish(1, down)
    arrive(far_side, 0)
    hand(far_side, 0, across)
    arrive(far_side, 1)
    hand(far_side, 1, across)
    arrive(up, 0)
    extras(up)
    finish(2, up)
    extras(across)
    finish(3, across)

    for step in range(1, n_x):
        src = (row_x + step) % n_x
        remote(pb_rcv.at[src], pb_rcv.at[src], pb_ss.at[0], pb_rs.at[src], x_id(step)).wait_recv()
    piece = pb_rcv[0]
    for d in range(1, n_x):
        piece = piece + pb_rcv[d]
    pf_rcv[me] = piece * (1.0 / total)
    pf_sends = []
    for step in range(1, NB):
        copy = remote(
            pf_rcv.at[me], pf_rcv.at[me], pf_ss.at[step], pf_rs.at[me], {"beam": peer(step)}
        )
        copy.start()
        pf_sends.append(copy)

    extras(far_side)
    finish(4, far_side)
    arrive(across_up, 0)
    arrive(across_up, 1)
    extras(across_up)
    finish(5, across_up)
    arrive(across_down, 0)
    arrive(across_down, 1)
    extras(across_down)
    finish(6, across_down)
    for step in range(1, NB):
        src = peer(step)
        remote(pf_rcv.at[src], pf_rcv.at[src], pf_ss.at[0], pf_rs.at[src], {"beam": src}).wait_recv()
    for d in range(NB):
        for g in range(8):
            start = (d % 4 * 8 + g) * 128
            probe_out[d // 4 : d // 4 + 1, start : start + 128] = pf_rcv[d, g : g + 1, :]
    arrive(across_far, 0)
    arrive(across_far, 1)
    extras(across_far)
    finish(7, across_far)

    for copy in tap_sends + u_sends + ow_sends + tg_sends + pr_sends + pa_sends + eg_sends + lg_sends + pb_sends + pf_sends:
        copy.wait_send()
    for order, block in enumerate(
        [me, down, up, across, far_side, across_up, across_down, across_far]
    ):
        out_copy(order, block).wait()


def hand_over(grad_hbm, probe_hbm, grad_out, probe_out, grad_v, probe_v, in_sems, out_sems):
    count = E // PART
    loads, stores = [], []
    for part in range(count):
        rows = pl.ds(part * PART, PART)
        loads.append(
            pltpu.make_async_copy(grad_hbm.at[rows], grad_v.at[rows], in_sems.at[part])
        )
        stores.append(
            pltpu.make_async_copy(grad_v.at[rows], grad_out.at[rows], out_sems.at[part])
        )
    loads.append(pltpu.make_async_copy(probe_hbm, probe_v, in_sems.at[count]))
    stores.append(pltpu.make_async_copy(probe_v, probe_out, out_sems.at[count]))
    for load in loads:
        load.start()
    for load, store in zip(loads, stores):
        load.wait()
        store.start()
    for store in stores:
        store.wait()


def body(
    sizes,
    densities,
    spectra,
    intensities,
    positions,
    probe,
    line_channels,
    line_weights,
    atten_coef,
    beta_coef,
    delta_coef,
):
    n_grp, n_row, n_x, n_zh, total = sizes
    chirps, right, left = constant_tables()
    dens = densities.reshape(E, NB, ZB * X, 128)
    spec = spectra.reshape(ZB * 128, C)
    vmem = pl.BlockSpec(memory_space=pltpu.VMEM)
    smem = pl.BlockSpec(memory_space=pltpu.SMEM)
    anywhere = pl.BlockSpec(memory_space=pl.ANY)
    n_near = n_grp * n_zh
    dma = pltpu.SemaphoreType.DMA
    small = (NB, 3, ZB, 128)
    out, probe_grad = pl.pallas_call(
        functools.partial(kernel, sizes),
        out_shape=(
            jax.ShapeDtypeStruct((E, NB, ZB * X, 128), BF16),
            jax.ShapeDtypeStruct((2, M * M), F32),
        ),
        in_specs=[
            anywhere,
            anywhere,
            anywhere,
            smem,
            vmem,
            vmem,
            vmem,
            smem,
            smem,
            smem,
            vmem,
            vmem,
            vmem,
        ],
        out_specs=(anywhere, vmem),
        scratch_shapes=[
            pltpu.VMEM((E, NB, ZB * X, 128), BF16),
            pltpu.VMEM((E, NB, ZB * X, 128), F32),
            pltpu.VMEM((ZB * 128, C), BF16),
            pltpu.VMEM((K, M * M), BF16),
            pltpu.VMEM((K * M, 128), F32),
            pltpu.VMEM((2, M, 128), F32),
            pltpu.VMEM(small, F32),
            pltpu.VMEM(small, F32),
            pltpu.VMEM((NB, 2, E, 8, 128), F32),
            pltpu.VMEM((NB, 2, E, 8, 128), F32),
            pltpu.VMEM(small, F32),
            pltpu.VMEM(small, F32),
            pltpu.VMEM((NB, X, ZB, 128), F32),
            pltpu.VMEM((NB, 2, ZB, 128), F32),
            pltpu.VMEM((NB, 2, ZB, 128), F32),
            pltpu.VMEM(small, F32),
            pltpu.VMEM(small, F32),
            pltpu.VMEM((NB, 2, E, 8, 128), F32),
            pltpu.VMEM((ZB * E, 128), F32),
            pltpu.VMEM((E, ZB * 128), F32),
            pltpu.VMEM((E, NB, ZB * X, 128), BF16),
            pltpu.VMEM((128, 256), F32),
            pltpu.VMEM((2, M, 128), F32),
            pltpu.VMEM((NB, 8, 128), F32),
            pltpu.VMEM((NB, 8, 128), F32),
            pltpu.VMEM((n_near, 8, 128), F32),
            pltpu.VMEM((n_x, 8, 128), F32),
            pltpu.VMEM((NB, 8, 128), F32),
            dma((NB,)),
            dma,
            dma,
            dma((NB,)),
            dma((NB,)),
            dma((NB,)),
            dma((NB, 2)),
            dma((NB, 2)),
            dma((NB,)),
            dma((NB,)),
            dma((NB,)),
            dma((NB,)),
            dma((NB,)),
            dma((NB,)),
            dma((14,)),
            dma((NB, 2)),
            dma((NB,)),
            dma((NB,)),
            dma((n_near,)),
            dma((n_near,)),
            dma((n_x,)),
            dma((n_x,)),
            dma((NB,)),
            dma((NB,)),
        ],
        compiler_params=pltpu.CompilerParams(
            collective_id=0, has_side_effects=True, vmem_limit_bytes=60 * 1024 * 1024
        ),
    )(
        dens,
        spec,
        intensities,
        positions.T,
        probe,
        line_channels.T,
        line_weights.T,
        atten_coef,
        beta_coef,
        delta_coef,
        jnp.asarray(chirps),
        jnp.asarray(right),
        jnp.asarray(left),
    )
    out, probe_grad = pl.pallas_call(
        hand_over,
        out_shape=(
            jax.ShapeDtypeStruct(out.shape, BF16),
            jax.ShapeDtypeStruct(probe_grad.shape, F32),
        ),
        in_specs=[anywhere, anywhere],
        out_specs=(anywhere, anywhere),
        scratch_shapes=[
            pltpu.VMEM(out.shape, BF16),
            pltpu.VMEM(probe_grad.shape, F32),
            dma((E // PART + 1,)),
            dma((E // PART + 1,)),
        ],
        compiler_params=pltpu.CompilerParams(vmem_limit_bytes=60 * 1024 * 1024),
    )(out, probe_grad)
    return out.reshape(densities.shape), probe_grad


def solution(mesh):
    n_grp, n_beam, n_row = mesh.shape["grp"], mesh.shape["beam"], mesh.shape["row"]
    n_zh = 4 if n_row % 4 == 0 else 1
    sizes = (n_grp, n_row, n_row // n_zh, n_zh, float(K * n_grp * n_beam * n_row))
    return jax.shard_map(
        functools.partial(body, sizes),
        mesh=mesh,
        in_specs=(
            P(None, "grp", "beam", "row"),
            P(("grp", "beam"), "row", None),
            P(("grp", "beam", "row"), None),
            P(("grp", "beam", "row"), None),
            P(),
            P(),
            P(),
            P(),
            P(),
            P(),
        ),
        out_specs=(P(None, "grp", "beam", "row"), P()),
        check_vma=False,
    )
```

profile of v0, /device:TPU:2, one launch (start us, length us, event | category | flops | bytes accessed | tf_op | source)
XLA Modules:
  0.0 70.4 jit_solution(16341853974498388378)
XLA Ops:
  0.6 66.2 %shard_map.140 = (bf16[32,8,64,128]{3,2,1,0:T(8,128)(2,1)}, f32[2,4096]{1,0:T(2,128)}) custom-call(bf16[32,8,64,128]{3,2,1,0:T(8,128)(2,1)} %bitcast.6, bf16[2048,512]{1,0:T(8,128)(2,1)} %bitcast.7, bf16[32,4096]{1,0:T(8,128)(2,1)} %inten_hbm.1, s32[2,32]{1,0:T(2,128)} %bitcast.10, f32[2,4096]{1,0:T(2,128)} %probe_ref.1, s32[4,32]{1,0:T(4,128)} %bitcast.8, ...), custom_call_target="tpu_custom_call" | custom-call | tf_op jit(solution)/shard_map/pallas_call | solution.py:796
  66.8 3.6 %shard_map.141 = (bf16[32,8,64,128]{3,2,1,0:T(8,128)(2,1)}, f32[2,4096]{1,0:T(2,128)}) custom-call(bf16[32,8,64,128]{3,2,1,0:T(8,128)(2,1)} %get-tuple-element.6.grad_hbm, f32[2,4096]{1,0:T(2,128)} %get-tuple-element.7.probe_hbm), custom_call_target="tpu_custom_call" | custom-call | tf_op jit(solution)/shard_map/pallas_call | solution.py:890
where the time goes:
time: 70.5 us; the launch traced here: 70.4 us
  Pallas kernels  69.8 us (99%)
    pallas_call x1, Pallas kernels, body(): pl.pallas_call(functools.partial(kernel, sizes), out_shape=(jax.ShapeDtyp...  66.2 us
    pallas_call x1, Pallas kernels, body(): pl.pallas_call(hand_over, out_shape=(jax.ShapeDtypeStruct(out.shape, BF16...  3.6 us

commit v1 on v0

--- a/solution.py
+++ b/solution.py
@@ -19,7 +19,7 @@
 GROUP = 16
 NEAREST = (4, 1, 7, 3, 5, 2, 6)
 ORDER = tuple((step, half) for half in range(2) for step in NEAREST)
-EARLY = 3
+EARLY = 7
 PART = 4
 
 F32 = jnp.float32
@@ -144,6 +144,7 @@
     pb_rs,
     pf_ss,
     pf_rs,
+    hello_sem,
 ):
     n_grp, n_row, n_x, n_zh, total = sizes
     me = lax.axis_index("beam")
@@ -174,12 +175,20 @@
         )
 
     barrier = pltpu.get_barrier_semaphore()
+    is_lead = me == 0
     for step in range(1, NB):
-        pl.semaphore_signal(barrier, inc=1, device_id={"beam": peer(step)}, device_id_type=MESH)
-    for step in range(1, n_near):
-        pl.semaphore_signal(barrier, inc=1, device_id=near_id(step), device_id_type=MESH)
-    for step in range(1, n_x):
-        pl.semaphore_signal(barrier, inc=1, device_id=x_id(step), device_id_type=MESH)
+        dst = peer(step)
+
+        @pl.when(dst != 0)
+        def _():
+            pl.semaphore_signal(barrier, inc=1, device_id={"beam": dst}, device_id_type=MESH)
+
+    @pl.when(is_lead)
+    def _():
+        for step in range(1, n_near):
+            pl.semaphore_signal(barrier, inc=1, device_id=near_id(step), device_id_type=MESH)
+        for step in range(1, n_x):
+            pl.semaphore_signal(barrier, inc=1, device_id=x_id(step), device_id_type=MESH)
 
     def dens_copy(step):
         block = (me + 1 + step) % NB
@@ -225,7 +234,15 @@
         return carry
 
     lax.fori_loop(0, NB, project, 0)
-    pl.semaphore_wait(barrier, NB - 1 + n_near - 1 + n_x - 1)
+    @pl.when(jnp.logical_not(is_lead))
+    def _():
+        pl.semaphore_wait(barrier, NB - 1)
+        pl.semaphore_signal(hello_sem, inc=1, device_id={"beam": 0}, device_id_type=MESH)
+
+    @pl.when(is_lead)
+    def _():
+        pl.semaphore_wait(hello_sem, NB - 1)
+
     tap_sends, u_sends = [], []
 
     def send_tap(step):
@@ -473,10 +490,9 @@
     half_first = first[: M // 2]
     flat_real = jnp.where(half_first, upper, swap(lower))
     flat_imag = jnp.where(half_first, swap(upper), lower)
-    for d in range(NB // 2):
-        pr_src[d] = flat_real[d * 8 : (d + 1) * 8]
-        pr_src[NB // 2 + d] = flat_imag[d * 8 : (d + 1) * 8]
-    tg_sends, pr_sends = [], []
+    pr_src[: M // 2] = flat_real
+    pr_src[M // 2 :] = flat_imag
+    tg_sends = []
     for step in range(1, NB):
         dst = peer(step)
         copy = remote(
@@ -484,15 +500,15 @@
         )
         copy.start()
         tg_sends.append(copy)
-    for step in range(1, NB):
-        dst = peer(step)
-        copy = remote(
-            pr_src.at[dst], pr_rcv.at[me], pr_ss.at[step], pr_rs.at[me], {"beam": dst}
-        )
-        copy.start()
-        pr_sends.append(copy)
+
+    def pr_copy(src):
+        return remote(pr_src, pr_rcv.at[src], pr_ss, pr_rs.at[src], {"beam": 0})
+
+    @pl.when(jnp.logical_not(is_lead))
+    def _():
+        pr_copy(me).start()
+
     tg_rcv[me] = tg_src[me]
-    pr_rcv[me] = pr_src[me]
 
     def scale_block(block, carry):
         for x in range(X):
@@ -570,20 +586,32 @@
     hand(me, 0, across)
     hand(me, 0, down)
     wait_u(1)
-    for step in range(1, NB):
-        src = peer(step)
-        remote(pr_src.at[src], pr_rcv.at[src], pr_ss.at[0], pr_rs.at[src], {"beam": src}).wait_recv()
-    piece = pr_rcv[0]
-    for d in range(1, NB):
-        piece = piece + pr_rcv[d]
-    pa_rcv[near] = piece
-    pa_sends = []
-    for step in range(1, n_near):
-        copy = remote(
-            pa_rcv.at[near], pa_rcv.at[near], pa_ss.at[step], pa_rs.at[near], near_id(step)
-        )
-        copy.start()
-        pa_sends.append(copy)
+
+    def pa_copy(step, owner):
+        return remote(
+            pa_rcv.at[owner], pa_rcv.at[owner], pa_ss.at[step], pa_rs.at[owner], near_id(step)
+        )
+
+    def pb_copy(step, owner):
+        return remote(
+            pb_rcv.at[owner], pb_rcv.at[owner], pb_ss.at[step], pb_rs.at[owner], x_id(step)
+        )
+
+    def pf_copy(step):
+        return remote(pf_rcv, pf_rcv, pf_ss.at[step], pf_rs, {"beam": peer(step)})
+
+    @pl.when(is_lead)
+    def _():
+        for src in range(1, NB):
+            pr_copy(src).wait_recv()
+        piece = pr_src[...]
+        for src in range(1, NB):
+            piece = piece + pr_rcv[src]
+        pa_rcv[near] = piece
+        pl.semaphore_wait(barrier, n_near - 1 + n_x - 1)
+        for step in range(1, n_near):
+            pa_copy(step, near).start()
+
     own_half(1)
     hand(me, 1, down)
     hand(me, 1, across)
@@ -675,21 +703,6 @@
     hand(across, 1, down)
     finish(0, me)
 
-    for step in range(1, n_near):
-        src = (near + step) % n_near
-        remote(pa_rcv.at[src], pa_rcv.at[src], pa_ss.at[0], pa_rs.at[src], near_id(step)).wait_recv()
-    piece = pa_rcv[0]
-    for d in range(1, n_near):
-        piece = piece + pa_rcv[d]
-    pb_rcv[row_x] = piece
-    pb_sends = []
-    for step in range(1, n_x):
-        copy = remote(
-            pb_rcv.at[row_x], pb_rcv.at[row_x], pb_ss.at[step], pb_rs.at[row_x], x_id(step)
-        )
-        copy.start()
-        pb_sends.append(copy)
-
     arrive(down, 1)
     extras(down)
     finish(1, down)
@@ -697,29 +710,38 @@
     hand(far_side, 0, across)
     arrive(far_side, 1)
     hand(far_side, 1, across)
+
+    @pl.when(is_lead)
+    def _():
+        for step in range(1, n_near):
+            pa_copy(step, (near + step) % n_near).wait_recv()
+        piece = pa_rcv[0]
+        for d in range(1, n_near):
+            piece = piece + pa_rcv[d]
+        pb_rcv[row_x] = piece
+        for step in range(1, n_x):
+            pb_copy(step, row_x).start()
+
     arrive(up, 0)
     extras(up)
     finish(2, up)
     extras(across)
     finish(3, across)
 
-    for step in range(1, n_x):
-        src = (row_x + step) % n_x
-        remote(pb_rcv.at[src], pb_rcv.at[src], pb_ss.at[0], pb_rs.at[src], x_id(step)).wait_recv()
-    piece = pb_rcv[0]
-    for d in range(1, n_x):
-        piece = piece + pb_rcv[d]
-    pf_rcv[me] = piece * (1.0 / total)
-    pf_sends = []
-    for step in range(1, NB):
-        copy = remote(
-            pf_rcv.at[me], pf_rcv.at[me], pf_ss.at[step], pf_rs.at[me], {"beam": peer(step)}
-        )
-        copy.start()
-        pf_sends.append(copy)
-
     extras(far_side)
     finish(4, far_side)
+
+    @pl.when(is_lead)
+    def _():
+        for step in range(1, n_x):
+            pb_copy(step, (row_x + step) % n_x).wait_recv()
+        piece = pb_rcv[0]
+        for d in range(1, n_x):
+            piece = piece + pb_rcv[d]
+        pf_rcv[...] = piece * (1.0 / total)
+        for step in range(1, NB):
+            pf_copy(step).start()
+
     arrive(across_up, 0)
     arrive(across_up, 1)
     extras(across_up)
@@ -728,20 +750,37 @@
     arrive(across_down, 1)
     extras(across_down)
     finish(6, across_down)
-    for step in range(1, NB):
-        src = peer(step)
-        remote(pf_rcv.at[src], pf_rcv.at[src], pf_ss.at[0], pf_rs.at[src], {"beam": src}).wait_recv()
-    for d in range(NB):
-        for g in range(8):
-            start = (d % 4 * 8 + g) * 128
-            probe_out[d // 4 : d // 4 + 1, start : start + 128] = pf_rcv[d, g : g + 1, :]
+
     arrive(across_far, 0)
     arrive(across_far, 1)
     extras(across_far)
     finish(7, across_far)
 
-    for copy in tap_sends + u_sends + ow_sends + tg_sends + pr_sends + pa_sends + eg_sends + lg_sends + pb_sends + pf_sends:
+    @pl.when(jnp.logical_not(is_lead))
+    def _():
+        pf_copy(1).wait_recv()
+
+    for part in range(2):
+        for g in range(M // 2):
+            row_at = part * (M // 2) + g
+            probe_out[part : part + 1, g * 128 : (g + 1) * 128] = pf_rcv[row_at : row_at + 1, :]
+
+    for copy in tap_sends + u_sends + ow_sends + tg_sends + eg_sends + lg_sends:
         copy.wait_send()
+
+    @pl.when(jnp.logical_not(is_lead))
+    def _():
+        pr_copy(me).wait_send()
+
+    @pl.when(is_lead)
+    def _():
+        for step in range(1, n_near):
+            pa_copy(step, near).wait_send()
+        for step in range(1, n_x):
+            pb_copy(step, row_x).wait_send()
+        for step in range(1, NB):
+            pf_copy(step).wait_send()
+
     for order, block in enumerate(
         [me, down, up, across, far_side, across_up, across_down, across_far]
     ):
@@ -839,11 +878,11 @@
             pltpu.VMEM((E, NB, ZB * X, 128), BF16),
             pltpu.VMEM((128, 256), F32),
             pltpu.VMEM((2, M, 128), F32),
-            pltpu.VMEM((NB, 8, 128), F32),
-            pltpu.VMEM((NB, 8, 128), F32),
-            pltpu.VMEM((n_near, 8, 128), F32),
-            pltpu.VMEM((n_x, 8, 128), F32),
-            pltpu.VMEM((NB, 8, 128), F32),
+            pltpu.VMEM((M, 128), F32),
+            pltpu.VMEM((NB, M, 128), F32),
+            pltpu.VMEM((n_near, M, 128), F32),
+            pltpu.VMEM((n_x, M, 128), F32),
+            pltpu.VMEM((M, 128), F32),
             dma((NB,)),
             dma,
             dma,
@@ -860,14 +899,15 @@
             dma((NB,)),
             dma((14,)),
             dma((NB, 2)),
-            dma((NB,)),
+            dma,
             dma((NB,)),
             dma((n_near,)),
             dma((n_near,)),
             dma((n_x,)),
             dma((n_x,)),
             dma((NB,)),
-            dma((NB,)),
+            dma,
+            pltpu.SemaphoreType.REGULAR,
         ],
         compiler_params=pltpu.CompilerParams(
             collective_id=0, has_side_effects=True, vmem_limit_bytes=60 * 1024 * 1024

time: 70.5 us -> 66.9 us (0.949)
  the two profiles are of different devices: /device:TPU:2 before, /device:TPU:120 now
where the time goes in v1:
time: 66.9 us; the launch traced here: 66.8 us
  Pallas kernels  66.1 us (99%)
    pallas_call x1, Pallas kernels, body(): pl.pallas_call(functools.partial(kernel, sizes), out_shape=(jax.ShapeDtyp...  62.5 us
    pallas_call x1, Pallas kernels, body(): pl.pallas_call(hand_over, out_shape=(jax.ShapeDtypeStruct(out.shape, BF16...  3.6 us

profile of v1, /device:TPU:120, one launch (start us, length us, event | category | flops | bytes accessed | tf_op | source)
XLA Modules:
  0.0 66.8 jit_solution(13312673463024543148)
XLA Ops:
  0.6 62.5 %shard_map.140 = (bf16[32,8,64,128]{3,2,1,0:T(8,128)(2,1)}, f32[2,4096]{1,0:T(2,128)}) custom-call(bf16[32,8,64,128]{3,2,1,0:T(8,128)(2,1)} %bitcast.6, bf16[2048,512]{1,0:T(8,128)(2,1)} %bitcast.7, bf16[32,4096]{1,0:T(8,128)(2,1)} %inten_hbm.1, s32[2,32]{1,0:T(2,128)} %bitcast.10, f32[2,4096]{1,0:T(2,128)} %probe_ref.1, s32[4,32]{1,0:T(4,128)} %bitcast.8, ...), custom_call_target="tpu_custom_call" | custom-call | tf_op jit(solution)/shard_map/pallas_call | solution.py:835
  63.2 3.6 %shard_map.141 = (bf16[32,8,64,128]{3,2,1,0:T(8,128)(2,1)}, f32[2,4096]{1,0:T(2,128)}) custom-call(bf16[32,8,64,128]{3,2,1,0:T(8,128)(2,1)} %get-tuple-element.6.grad_hbm, f32[2,4096]{1,0:T(2,128)} %get-tuple-element.7.probe_hbm), custom_call_target="tpu_custom_call" | custom-call | tf_op jit(solution)/shard_map/pallas_call | solution.py:930

commit v2 on v1

--- a/solution.py
+++ b/solution.py
@@ -613,9 +613,6 @@
             pa_copy(step, near).start()
 
     own_half(1)
-    hand(me, 1, down)
-    hand(me, 1, across)
-    hand(me, 1, up)
 
     def weigh(e, sums):
         value = jnp.concatenate([eg_ref[me, 0, e], eg_ref[me, 1, e]], 0)
@@ -653,6 +650,10 @@
         lg_sends.append(copy)
     lg_rcv[me] = lg_src[me]
 
+    hand(me, 1, down)
+    hand(me, 1, across)
+    hand(me, 1, up)
+
     def out_copy(order, block):
         return pltpu.make_async_copy(
             out_v.at[:, block], out_hbm.at[:, block], out_sem.at[order]
@@ -703,14 +704,6 @@
     hand(across, 1, down)
     finish(0, me)
 
-    arrive(down, 1)
-    extras(down)
-    finish(1, down)
-    arrive(far_side, 0)
-    hand(far_side, 0, across)
-    arrive(far_side, 1)
-    hand(far_side, 1, across)
-
     @pl.when(is_lead)
     def _():
         for step in range(1, n_near):
@@ -721,6 +714,14 @@
         pb_rcv[row_x] = piece
         for step in range(1, n_x):
             pb_copy(step, row_x).start()
+
+    arrive(down, 1)
+    extras(down)
+    finish(1, down)
+    arrive(far_side, 0)
+    hand(far_side, 0, across)
+    arrive(far_side, 1)
+    hand(far_side, 1, across)
 
     arrive(up, 0)
     extras(up)

time: 66.9 us -> 66.8 us (level)
  the two profiles are of different devices: /device:TPU:120 before, /device:TPU:2 now
where the time goes in v2:
time: 66.8 us; the launch traced here: 65.8 us
  Pallas kernels  65.2 us (98%)
    pallas_call x1, Pallas kernels, body(): pl.pallas_call(functools.partial(kernel, sizes), out_shape=(jax.ShapeDtyp...  61.6 us
    pallas_call x1, Pallas kernels, body(): pl.pallas_call(hand_over, out_shape=(jax.ShapeDtypeStruct(out.shape, BF16...  3.6 us

profile of v2, /device:TPU:2, one launch (start us, length us, event | category | flops | bytes accessed | tf_op | source)
XLA Modules:
  0.0 65.8 jit_solution(256481889285660574)
XLA Ops:
  0.6 61.6 %shard_map.140 = (bf16[32,8,64,128]{3,2,1,0:T(8,128)(2,1)}, f32[2,4096]{1,0:T(2,128)}) custom-call(bf16[32,8,64,128]{3,2,1,0:T(8,128)(2,1)} %bitcast.6, bf16[2048,512]{1,0:T(8,128)(2,1)} %bitcast.7, bf16[32,4096]{1,0:T(8,128)(2,1)} %inten_hbm.1, s32[2,32]{1,0:T(2,128)} %bitcast.10, f32[2,4096]{1,0:T(2,128)} %probe_ref.1, s32[4,32]{1,0:T(4,128)} %bitcast.8, ...), custom_call_target="tpu_custom_call" | custom-call | tf_op jit(solution)/shard_map/pallas_call | solution.py:836
  62.2 3.6 %shard_map.141 = (bf16[32,8,64,128]{3,2,1,0:T(8,128)(2,1)}, f32[2,4096]{1,0:T(2,128)}) custom-call(bf16[32,8,64,128]{3,2,1,0:T(8,128)(2,1)} %get-tuple-element.6.grad_hbm, f32[2,4096]{1,0:T(2,128)} %get-tuple-element.7.probe_hbm), custom_call_target="tpu_custom_call" | custom-call | tf_op jit(solution)/shard_map/pallas_call | solution.py:931
